TPU v7x, 32 devices: a whole 2x2x4 slice. The times are simulated.
32 devices in a mesh: grp: 4 (over y, x), mem: 8 (over z, core).
Axes of the slice: x: 2, y: 2, z: 4, core: 2. Of those that a mesh axis runs over, the one named last changes fastest.
Arguments:
- embedding: bfloat16 [32768, 768], P(('grp', 'mem')), parts along dimension 0, may hold values from -127 to 127, as said below
- row_scale: float32 [32768], P(('grp', 'mem')), parts along dimension 0, may hold values from 0.0004 to 0.0006
- block_rows: int32 [64], P(('grp', 'mem')), parts along dimension 0, may hold values from 1 to 512, 6144 in all
- requests: int32 [32, 8], P(('grp', 'mem')), parts along dimension 0, may hold values from 0 to 1
Outputs:
- highest: float32 [32768], P(('grp', 'mem')), parts along dimension 0
There are 4 independent parts, one for each index of `grp`. A program takes and returns all parts, laid end to end along the dimension named above; each array names one. Nothing has to cross between parts.
Inputs may be any that keep to these rules, and one draw needn't show every extreme that they name: `embedding`: whole numbers, held exactly. `block_rows`: the largest block holds exactly 512 live rows.
All inputs are finite; a program needn't handle non-finite values.
Results may differ from a plain program's by a relative error of at most 0.0012.
Values may be sent and summed in bfloat16 or wider, within the bound.
A program may use at most 128 MiB of HBM per device.

v0:
```python
import jax
import jax.numpy as jnp
from jax import lax
from jax.sharding import PartitionSpec as P

BLOCK = 512


def shards(embedding, row_scale, block_rows, requests):
    members = lax.axis_size("mem")
    myself = lax.axis_index("mem")
    blocks_here = block_rows.shape[0]
    width = embedding.shape[1]
    decoded = (embedding.astype(jnp.float32) * row_scale[:, None]).astype(jnp.bfloat16)
    decoded = decoded.reshape(blocks_here, BLOCK, width)
    positions = jnp.arange(BLOCK, dtype=jnp.int32)
    local_live = positions[None, :] < block_rows[:, None]
    all_rows = lax.all_gather(block_rows, "mem", axis=0, tiled=True)
    wanted = lax.all_to_all(requests, "mem", split_axis=1, concat_axis=0, tiled=True)[:, 0]
    chosen = requests[0]
    local_ids = jnp.arange(blocks_here, dtype=jnp.int32)
    identity = positions[:, None] == positions[None, :]
    row_init = jnp.full((blocks_here, BLOCK), -1e30, dtype=jnp.float32)
    outgoing = jnp.take(decoded, wanted, axis=0)
    fetched = lax.all_to_all(outgoing, "mem", split_axis=0, concat_axis=0, tiled=True)
    owners = jnp.arange(members, dtype=jnp.int32)
    columns_live = positions[None, :] < all_rows[owners * blocks_here + chosen][:, None]
    own_block = jnp.where(owners == myself, chosen, -1)

    def visit(running, entries):
        partner, columns, own_index = entries
        scores = jnp.einsum("arc,sc->ars", decoded, partner, preferred_element_type=jnp.float32)
        diagonal = (local_ids[:, None, None] == own_index) & identity[None, :, :]
        allowed = columns[None, None, :] & jnp.logical_not(diagonal)
        masked = jnp.where(allowed, scores, jnp.float32(-1e30))
        running = jnp.maximum(running, jnp.max(masked, axis=2))
        column = jnp.max(jnp.where(local_live[:, :, None], masked, jnp.float32(-1e30)), axis=(0, 1))
        return (running, column)

    row_best, col_best = lax.scan(visit, row_init, (fetched, columns_live, own_block))
    returned = lax.all_to_all(col_best, "mem", split_axis=0, concat_axis=0, tiled=True)
    matches = wanted[None, :, None] == local_ids[:, None, None]
    incoming = jnp.max(jnp.where(matches, returned[None, :, :], jnp.float32(-1e30)), axis=1)
    highest = jnp.maximum(row_best, incoming)
    return jnp.where(local_live, highest, jnp.float32(0.0)).reshape(-1)


def solution(mesh):
    return jax.shard_map(
        shards,
        mesh=mesh,
        in_specs=(
            P(("grp", "mem"), None),
            P(("grp", "mem")),
            P(("grp", "mem")),
            P(("grp", "mem"), None),
        ),
        out_specs=P(("grp", "mem")),
        check_vma=False,
    )
```

profile of v0, /device:TPU:0, one launch (start us, length us, event | category | flops | bytes accessed | tf_op | source)
XLA Modules:
  0.0 209.2 jit_solution(18187052940408621945)
XLA Ops:
  0.0 1.3 copy.7
  1.3 6.3 %all-to-all-start = ((s32[1,8,1]{2,0,1:T(1,128)}), s32[1,8,1]{2,0,1:T(1,128)S(1)}, u32[]{:S(2)}, u32[]{:S(2)}) async-start(s32[1,8,1]{2,0,1:T(1,128)} %copy.7), calls=%async_computation | async-start | bytes 8192 | tf_op jit(solution)/shard_map/all_to_all | solution.py:19
  7.6 1.7 multiply_convert_fusion
  9.4 3.7 %all-to-all-done = s32[1,8,1]{2,0,1:T(1,128)S(1)} async-done(((s32[1,8,1]{2,0,1:T(1,128)}), s32[1,8,1]{2,0,1:T(1,128)S(1)}, u32[]{:S(2)}, u32[]{:S(2)}) %all-to-all-start) | async-done | bytes 64 | tf_op jit(solution)/shard_map/all_to_all | solution.py:19
  13.4 3.6 %gather_fusion.1 = bf16[8,512,768]{2,1,0:T(8,128)(2,1)} fusion(bf16[2,512,768]{2,1,0:T(8,128)(2,1)S(1)} %bitcast.40, s32[1024]{0:T(1024)S(1)} %pad_clamp_fusion), kind=kCustom, calls=%fused_computation.1 | custom fusion | bytes 12582944 | tf_op jit(solution)/shard_map/jit(_take)/gather | solution.py:24
  17.0 6.1 %broadcast_select_fusion = bf16[8,512,768]{2,1,0:T(8,128)(2,1)} fusion(bf16[8,512,768]{2,1,0:T(8,128)(2,1)} %gather_fusion.1, pred[8]{0:T(512)(128)(4,1)S(1)} %compare_and_fusion), kind=kLoop, calls=%fused_computation.15 | loop fusion | flops 3145728 | bytes 12582920 | tf_op jit(solution)/shard_map/jit(_take)/select_n | solution.py:24
  23.1 4.9 %all-to-all-start.1 = ((bf16[8,512,768]{2,1,0:T(8,128)(2,1)}), bf16[8,512,768]{2,1,0:T(8,128)(2,1)}, u32[]{:S(2)}, u32[]{:S(2)}) async-start(bf16[8,512,768]{2,1,0:T(8,128)(2,1)} %broadcast_select_fusion), calls=%async_computation.1 | async-start | bytes 12582912 | tf_op jit(solution)/shard_map/all_to_all | solution.py:25
  28.0 0.6 dynamic-slice
  29.5 137.6 %all-reduce = s32[16]{0:T(128)S(1)} all-reduce(s32[16]{0:T(128)S(1)} %dynamic-update-slice), channel_id=1, replica_groups=mesh['grp'=4,'mem'=8] {'mem'}, use_global_device_ids=true, to_apply=%add | all-reduce | flops 16 | bytes 128
  167.1 0.6 gather_fusion
  167.8 31.0 %while.13 = (s32[]{:T(128)}, f32[2,512]{1,0:T(2,128)S(1)}, f32[8,512]{1,0:T(8,128)S(1)}, pred[8,512]{1,0:T(8,128)(4,1)S(1)}, s32[8]{0:T(128)S(1)}, /*index=5*/bf...) while((s32[]{:T(128)}, f32[2,512]{1,0:T(2,128)S(1)}, ...), condition=%wide.region_3.4_spmd.clone, body=%wide.region_0.3_spmd.clone.sunk | while | flops 809240064 | bytes 2910355 | solution.py:40
  169.2 2.4 %select_reduce_fusion.3 = (f32[512]{0:T(512)S(1)}, f32[2,512]{1,0:T(2,128)S(1)}) fusion(pred[2,512]{1,0:T(4,128)(4,1)S(1)} %iota_compare_fusion.8, bf16[2,512,768]{2,1,0:T(8,128)(2,1)S(1)} %get-tuple-element.191, bf16[8,512,768]{2,1,0:T(8,128)(2,1)} %get-tuple-element.190, s32[]{:T(128)} %get-tuple-element.175, ...), kind=kOutput, calls=%fused_computation.6.clone.1 | convolution fusion | flops 808974848 | bytes 2629634 | tf_op jit(solution)/shard_map/while/body/eval_jaxpr/arc,sc->ars/dot_general | solution.py:32
  171.7 0.6 dynamic_slice.27
  173.1 2.4 %select_reduce_fusion.3 = (f32[512]{0:T(512)S(1)}, f32[2,512]{1,0:T(2,128)S(1)}) fusion(pred[2,512]{1,0:T(4,128)(4,1)S(1)} %iota_compare_fusion.8, bf16[2,512,768]{2,1,0:T(8,128)(2,1)S(1)} %get-tuple-element.191, bf16[8,512,768]{2,1,0:T(8,128)(2,1)} %get-tuple-element.190, s32[]{:T(128)} %get-tuple-element.175, ...), kind=kOutput, calls=%fused_computation.6.clone.1 | convolution fusion | flops 808974848 | bytes 2629634 | tf_op jit(solution)/shard_map/while/body/eval_jaxpr/arc,sc->ars/dot_general | solution.py:32
  177.0 2.4 %select_reduce_fusion.3 = (f32[512]{0:T(512)S(1)}, f32[2,512]{1,0:T(2,128)S(1)}) fusion(pred[2,512]{1,0:T(4,128)(4,1)S(1)} %iota_compare_fusion.8, bf16[2,512,768]{2,1,0:T(8,128)(2,1)S(1)} %get-tuple-element.191, bf16[8,512,768]{2,1,0:T(8,128)(2,1)} %get-tuple-element.190, s32[]{:T(128)} %get-tuple-element.175, ...), kind=kOutput, calls=%fused_computation.6.clone.1 | convolution fusion | flops 808974848 | bytes 2629634 | tf_op jit(solution)/shard_map/while/body/eval_jaxpr/arc,sc->ars/dot_general | solution.py:32
  180.8 2.4 %select_reduce_fusion.3 = (f32[512]{0:T(512)S(1)}, f32[2,512]{1,0:T(2,128)S(1)}) fusion(pred[2,512]{1,0:T(4,128)(4,1)S(1)} %iota_compare_fusion.8, bf16[2,512,768]{2,1,0:T(8,128)(2,1)S(1)} %get-tuple-element.191, bf16[8,512,768]{2,1,0:T(8,128)(2,1)} %get-tuple-element.190, s32[]{:T(128)} %get-tuple-element.175, ...), kind=kOutput, calls=%fused_computation.6.clone.1 | convolution fusion | flops 808974848 | bytes 2629634 | tf_op jit(solution)/shard_map/while/body/eval_jaxpr/arc,sc->ars/dot_general | solution.py:32
  184.7 2.4 %select_reduce_fusion.3 = (f32[512]{0:T(512)S(1)}, f32[2,512]{1,0:T(2,128)S(1)}) fusion(pred[2,512]{1,0:T(4,128)(4,1)S(1)} %iota_compare_fusion.8, bf16[2,512,768]{2,1,0:T(8,128)(2,1)S(1)} %get-tuple-element.191, bf16[8,512,768]{2,1,0:T(8,128)(2,1)} %get-tuple-element.190, s32[]{:T(128)} %get-tuple-element.175, ...), kind=kOutput, calls=%fused_computation.6.clone.1 | convolution fusion | flops 808974848 | bytes 2629634 | tf_op jit(solution)/shard_map/while/body/eval_jaxpr/arc,sc->ars/dot_general | solution.py:32
  188.6 2.4 %select_reduce_fusion.3 = (f32[512]{0:T(512)S(1)}, f32[2,512]{1,0:T(2,128)S(1)}) fusion(pred[2,512]{1,0:T(4,128)(4,1)S(1)} %iota_compare_fusion.8, bf16[2,512,768]{2,1,0:T(8,128)(2,1)S(1)} %get-tuple-element.191, bf16[8,512,768]{2,1,0:T(8,128)(2,1)} %get-tuple-element.190, s32[]{:T(128)} %get-tuple-element.175, ...), kind=kOutput, calls=%fused_computation.6.clone.1 | convolution fusion | flops 808974848 | bytes 2629634 | tf_op jit(solution)/shard_map/while/body/eval_jaxpr/arc,sc->ars/dot_general | solution.py:32
  192.5 2.4 %select_reduce_fusion.3 = (f32[512]{0:T(512)S(1)}, f32[2,512]{1,0:T(2,128)S(1)}) fusion(pred[2,512]{1,0:T(4,128)(4,1)S(1)} %iota_compare_fusion.8, bf16[2,512,768]{2,1,0:T(8,128)(2,1)S(1)} %get-tuple-element.191, bf16[8,512,768]{2,1,0:T(8,128)(2,1)} %get-tuple-element.190, s32[]{:T(128)} %get-tuple-element.175, ...), kind=kOutput, calls=%fused_computation.6.clone.1 | convolution fusion | flops 808974848 | bytes 2629634 | tf_op jit(solution)/shard_map/while/body/eval_jaxpr/arc,sc->ars/dot_general | solution.py:32
  196.4 2.4 %select_reduce_fusion.3 = (f32[512]{0:T(512)S(1)}, f32[2,512]{1,0:T(2,128)S(1)}) fusion(pred[2,512]{1,0:T(4,128)(4,1)S(1)} %iota_compare_fusion.8, bf16[2,512,768]{2,1,0:T(8,128)(2,1)S(1)} %get-tuple-element.191, bf16[8,512,768]{2,1,0:T(8,128)(2,1)} %get-tuple-element.190, s32[]{:T(128)} %get-tuple-element.175, ...), kind=kOutput, calls=%fused_computation.6.clone.1 | convolution fusion | flops 808974848 | bytes 2629634 | tf_op jit(solution)/shard_map/while/body/eval_jaxpr/arc,sc->ars/dot_general | solution.py:32
  198.9 0.6 all_to_all.22
  199.5 3.3 %all-to-all-start.2 = ((f32[8,1,512]{2,1,0:T(1,128)}), f32[8,1,512]{2,1,0:T(1,128)S(1)}, u32[]{:S(2)}, u32[]{:S(2)}) async-start(f32[8,1,512]{2,1,0:T(1,128)} %all_to_all.22), calls=%async_computation.2 | async-start | bytes 32768 | tf_op jit(solution)/shard_map/all_to_all | solution.py:41
  202.8 5.6 %all-to-all-done.2 = f32[8,1,512]{2,1,0:T(1,128)S(1)} async-done(((f32[8,1,512]{2,1,0:T(1,128)}), f32[8,1,512]{2,1,0:T(1,128)S(1)}, u32[]{:S(2)}, u32[]{:S(2)}) %all-to-all-start.2) | async-done | bytes 16416 | tf_op jit(solution)/shard_map/all_to_all | solution.py:41
  208.6 0.6 copy.9
  (78 shorter events, 11.6 us)
Async XLA Ops:
  1.3 11.8 %all-to-all-start = ((s32[1,8,1]{2,0,1:T(1,128)}), s32[1,8,1]{2,0,1:T(1,128)S(1)}, u32[]{:S(2)}, u32[]{:S(2)}) async-start(s32[1,8,1]{2,0,1:T(1,128)} %copy.7), calls=%async_computation | async-start | bytes 8192 | tf_op jit(solution)/shard_map/all_to_all | solution.py:19
  23.1 4.9 %copy-start.2 = (u32[32]{0:T(128)S(1)}, u32[32]{0:T(128)}, u32[]{:S(2)}) copy-start(u32[32]{0:T(128)} %constant.54) | copy-start | bytes 388
  23.1 6.2 %copy-start = (s32[2]{0:T(128)S(1)}, s32[2]{0:T(128)}, u32[]{:S(2)}) copy-start(s32[2]{0:T(128)} %param.8) | copy-start | bytes 28
  23.1 144.0 %copy-start.1 = (s32[1,8]{1,0:T(1,128)S(1)}, s32[1,8]{1,0:T(1,128)}, u32[]{:S(2)}) copy-start(s32[1,8]{1,0:T(1,128)} %param.9) | copy-start | bytes 100
  23.1 144.7 %all-to-all-start.1 = ((bf16[8,512,768]{2,1,0:T(8,128)(2,1)}), bf16[8,512,768]{2,1,0:T(8,128)(2,1)}, u32[]{:S(2)}, u32[]{:S(2)}) async-start(bf16[8,512,768]{2,1,0:T(8,128)(2,1)} %broadcast_select_fusion), calls=%async_computation.1 | async-start | bytes 12582912 | tf_op jit(solution)/shard_map/all_to_all | solution.py:25
  199.5 8.9 %all-to-all-start.2 = ((f32[8,1,512]{2,1,0:T(1,128)}), f32[8,1,512]{2,1,0:T(1,128)S(1)}, u32[]{:S(2)}, u32[]{:S(2)}) async-start(f32[8,1,512]{2,1,0:T(1,128)} %all_to_all.22), calls=%async_computation.2 | async-start | bytes 32768 | tf_op jit(solution)/shard_map/all_to_all | solution.py:41
where the time goes:
time: 210 us; the launch traced here: 209 us
  blocking collectives  138 us (66%)
  matrix products  19.3 us (9%)
  starting transfers between devices  14.5 us (7%)
  other arithmetic  14.3 us (7%)
  local copies, waits for them, and re-layouts  13.1 us (6%)
  waiting for transfers between devices  9.32 us (4%)
    unnamed x1, blocking collectives  138 us
    dot_general x8, matrix products, visit(): jnp.einsum('arc,sc->ars', decoded, partner, preferred_element_type=jnp.fl...  19.3 us
    all_to_all x1, starting transfers between devices, shards(): lax.all_to_all(requests, 'mem', split_axis=1, concat_axis=0, tiled=True)  6.33 us
    select_n x2, other arithmetic, shards(): outgoing = jnp.take(decoded, wanted, axis=0)  6.11 us
    all_to_all x1, waiting for transfers between devices, shards(): lax.all_to_all(col_best, 'mem', split_axis=0, concat_axis=0, tiled=True)  5.57 us
    dynamic_slice x16, local copies, waits for them, and re-layouts, shards(): lax.scan(visit, row_init, (fetched, columns_live, own_block))  4.95 us
    all_to_all x1, starting transfers between devices, shards(): lax.all_to_all(outgoing, 'mem', split_axis=0, concat_axis=0, tiled=True)  4.87 us
    eq x8, other arithmetic, visit(): diagonal = (local_ids[:, None, None] == own_index) & identity[None, :, :]  4.61 us
  transfers between devices with their start and end apart: 3, of which 2 were waited for; matrix products, arithmetic and copies ran while one was open for 2% of the time, Pallas kernels for 0%

commit v1 on v0

--- a/solution.py
+++ b/solution.py
@@ -1,9 +1,15 @@
 import jax
 import jax.numpy as jnp
 from jax import lax
+from jax.experimental import pallas as pl
+from jax.experimental.pallas import tpu as pltpu
 from jax.sharding import PartitionSpec as P
 
 BLOCK = 512
+CHUNK = 64
+AHEAD = 4
+LOW = -1e30
+MESH = pl.DeviceIdType.MESH
 
 
 def shards(embedding, row_scale, block_rows, requests):
@@ -45,9 +51,365 @@
     return jnp.where(local_live, highest, jnp.float32(0.0)).reshape(-1)
 
 
+def scores_of(x, y):
+    return lax.dot_general(x, y, (((1,), (1,)), ((), ())), preferred_element_type=jnp.float32)
+
+
+def kernel(
+    rows_ref, own_ref, req_ref, out_ref,
+    chip, held, passing, other, best, out_x, out_y, reqs,
+    own_send, own_send2, held_send, passing_send, other_send, sib_send,
+    held_recv, passing_recv, other_recv, sib_recv, chip_sems,
+    best_recv, x_send, y_send, req_send, req_recv,
+):
+    grp, me = lax.axis_index("grp"), lax.axis_index("mem")
+    core, z = me % 2, me // 2
+    side = grp % 2
+    w = z + side * (3 - 2 * z)
+    pgrp = grp + 1 - 2 * side
+    sib = me + 1 - 2 * core
+    n_chunks = own_ref.shape[0] // CHUNK
+    half = n_chunks // 2
+
+    def at(group, pos, c):
+        s = side if group is grp else 1 - side
+        return (pos + s * (3 - 2 * pos)) * 2 + c
+
+    barrier = pltpu.get_barrier_semaphore()
+
+    def greet(i, _):
+        to = (me + 1 + i) % 8
+        pl.semaphore_signal(barrier, inc=1, device_id=(grp, to), device_id_type=MESH)
+        return 0
+
+    def greet_partner(i, _):
+        pl.semaphore_signal(barrier, inc=1, device_id=(pgrp, i), device_id_type=MESH)
+        return 0
+
+    lax.fori_loop(0, 7, greet, 0)
+    lax.fori_loop(0, 8, greet_partner, 0)
+    local = pltpu.make_async_copy(own_ref, chip.at[core], chip_sems.at[0])
+    local.start()
+    pl.semaphore_wait(barrier, 15)
+
+    def remote(src, dst, send, recv, group, to):
+        return pltpu.make_async_remote_copy(
+            src_ref=src, dst_ref=dst, send_sem=send, recv_sem=recv,
+            device_id=(group, to), device_id_type=MESH,
+        )
+
+    def part(k):
+        return pl.ds(pl.multiple_of(k * CHUNK, CHUNK), CHUNK)
+
+    def to_held(k):
+        return remote(own_ref.at[part(k)], held.at[part(k)], own_send.at[k], held_recv.at[k], grp, at(grp, w + 1, core))
+
+    def to_other_partner(k):
+        return remote(own_ref.at[part(k)], other.at[core, part(k)], own_send.at[k], other_recv.at[k], pgrp, me)
+
+    def to_other_left(k):
+        return remote(own_ref.at[part(k)], other.at[core, part(k)], own_send2.at[k], other_recv.at[k], grp, at(grp, 2, core))
+
+    def pass_held(k):
+        return remote(held.at[part(k)], passing.at[part(k)], held_send.at[k], passing_recv.at[k], pgrp, me)
+
+    def pass_on(k):
+        return remote(passing.at[part(k)], passing.at[part(k)], passing_send.at[k], passing_recv.at[k], grp, at(grp, w - 1, core))
+
+    def share(k):
+        return remote(other.at[core, part(k)], other.at[core, part(k)], other_send.at[k], sib_recv.at[k], grp, sib)
+
+    def take_share(k):
+        return remote(other.at[1 - core, part(k)], other.at[1 - core, part(k)], other_send.at[k], sib_recv.at[k], grp, sib)
+
+    def issue(k):
+        @pl.when(k < n_chunks)
+        def _():
+            @pl.when(w < 2)
+            def _():
+                to_held(k).start()
+
+            @pl.when(w >= 2)
+            def _():
+                to_other_partner(k).start()
+
+            @pl.when(w == 3)
+            def _():
+                to_other_left(k).start()
+
+    def loop(lo, hi, body):
+        def run(k, _):
+            body(k)
+            return 0
+        lax.fori_loop(lo, hi, run, 0)
+
+    swap = remote(own_ref, chip.at[core], sib_send.at[0], chip_sems.at[1], grp, sib)
+    swapped = remote(own_ref, chip.at[1 - core], sib_send.at[0], chip_sems.at[1], grp, sib)
+    swap.start()
+    loop(0, AHEAD, issue)
+
+    def req_copy(i):
+        to = (me + 1 + i) % 8
+        return remote(req_ref, reqs.at[me], req_send.at[i], req_recv.at[me], grp, to)
+
+    loop(0, 7, lambda i: req_copy(i).start())
+
+    def block(ref, lead, i):
+        rows = pl.ds(pl.multiple_of(i * BLOCK, BLOCK), BLOCK)
+        return ref[rows, :] if lead is None else ref[lead, rows, :]
+
+    def inside(dev):
+        def one(t):
+            a, b = t % 2, t // 2
+            s = scores_of(block(chip, dev, b), block(chip, core, a))
+            r = lax.broadcasted_iota(jnp.int32, s.shape, 0)
+            c = lax.broadcasted_iota(jnp.int32, s.shape, 1)
+            same = jnp.logical_and(dev == core, a == b).astype(jnp.int32)
+            limit = same * rows_ref[b] + (1 - same) * BLOCK
+            drop = (r >= limit) | ((r - c) * same + (1 - same) == 0)
+            best[dev + me - core, t] = jnp.max(jnp.where(drop, LOW, s), axis=0, keepdims=True)
+        loop(0, 4, one)
+
+    def cross(x, lead, i, ys, j0, n, stage):
+        def one(t):
+            yd, j = t % 2, j0 + t // 2
+            s = scores_of(block(x, lead, i), block(ys, yd, j))
+            out_y[stage, yd, i * 2 + j] = jnp.max(s, axis=0, keepdims=True)
+            m = s[:, :128]
+            for q in range(1, BLOCK // 128):
+                m = jnp.maximum(m, s[:, q * 128:(q + 1) * 128])
+            out_x[stage, yd, j * 2 + i] = jnp.max(m.T, axis=0, keepdims=True)
+        loop(0, 2 * n, one)
+
+    def x_back(stage, group, xid, yid, yd):
+        return remote(out_x.at[stage, yd], best.at[yid], x_send.at[stage, yd], best_recv.at[yid], group, xid)
+
+    def y_back(stage, group, xid, yid, yd):
+        return remote(out_y.at[stage, yd], best.at[xid], y_send.at[stage, yd], best_recv.at[xid], group, yid)
+
+    def chip_back(start):
+        xid = at(grp, w - 1, core)
+        ops = [x_back(0, grp, xid, at(grp, w, yd), yd) for yd in range(2)]
+        ops.append(y_back(0, grp, xid, sib, 1 - core))
+        for op in ops:
+            op.start() if start else op.wait_send()
+        if start:
+            best[xid] = out_y[0, core]
+
+    def pass_back(start):
+        xid, pos = at(pgrp, 0, core), 3 - w
+        for yd in range(2):
+            yid = at(pgrp, pos, yd)
+            for op in (x_back(1, pgrp, xid, yid, yd), y_back(1, pgrp, xid, yid, yd)):
+                op.start() if start else op.wait_send()
+
+    def far_back(start):
+        xid = at(grp, 1, core)
+        for yd in range(2):
+            yid = at(grp, 3, yd)
+            ops = (x_back(1, grp, xid, yid, yd), y_back(1, grp, xid, yid, yd), y_back(2, grp, me, yid, yd))
+            for op in ops:
+                op.start() if start else op.wait_send()
+            if start:
+                best[yid] = out_x[2, yd]
+
+    def shares(lo, hi):
+        loop(lo, hi, lambda k: take_share(k).wait_recv())
+
+    def step0(s):
+        issue(s + AHEAD)
+
+        @pl.when(s < n_chunks)
+        def _():
+            to_other_partner(s).wait_recv()
+            share(s).start()
+
+        @pl.when(s >= 3)
+        def _():
+            pass_on(s - 3).wait_recv()
+
+    def step1(s):
+        issue(s + AHEAD)
+
+        @pl.when(s < n_chunks)
+        def _():
+            to_held(s).wait_recv()
+            pass_held(s).start()
+            to_other_partner(s).wait_recv()
+            share(s).start()
+
+        @pl.when(s >= 2)
+        def _():
+            pass_on(s - 2).wait_recv()
+            pass_on(s - 2).start()
+
+    def step2(s):
+        issue(s + AHEAD)
+
+        @pl.when(s >= 1)
+        def _():
+            pass_held(s - 1).wait_recv()
+            pass_on(s - 1).start()
+
+        @pl.when(s < n_chunks)
+        def _():
+            to_other_left(s).wait_recv()
+            share(s).start()
+            to_held(s).wait_recv()
+
+    local.wait()
+    inside(core)
+    swapped.wait_recv()
+
+    @pl.when(w == 0)
+    def _():
+        inside(1 - core)
+        loop(0, half + 4, step0)
+        shares(0, half)
+        cross(passing, None, 0, other, 0, 1, 1)
+        loop(half + 4, n_chunks + 1, step0)
+        shares(half, n_chunks)
+        cross(passing, None, 0, other, 1, 1, 1)
+        loop(n_chunks + 1, n_chunks + 3, step0)
+        cross(passing, None, 1, other, 0, 2, 1)
+        pass_back(True)
+        loop(0, n_chunks, lambda k: to_held(k).wait_send())
+        loop(0, n_chunks, lambda k: share(k).wait_send())
+        pass_back(False)
+
+    @pl.when(w == 1)
+    def _():
+        inside(1 - core)
+        loop(0, half, step1)
+        cross(held, None, 0, chip, 0, 2, 0)
+        loop(half, half + 4, step1)
+        shares(0, half)
+        cross(passing, None, 0, other, 0, 1, 1)
+        loop(half + 4, n_chunks, step1)
+        cross(held, None, 1, chip, 0, 1, 0)
+        loop(n_chunks, n_chunks + 1, step1)
+        cross(held, None, 1, chip, 1, 1, 0)
+        chip_back(True)
+        loop(n_chunks + 1, n_chunks + 2, step1)
+        shares(half, n_chunks)
+        cross(passing, None, 0, other, 1, 1, 1)
+        cross(passing, None, 1, other, 0, 2, 1)
+        pass_back(True)
+        loop(0, n_chunks, lambda k: to_held(k).wait_send())
+        loop(0, n_chunks, lambda k: pass_held(k).wait_send())
+        loop(0, n_chunks, lambda k: pass_on(k).wait_send())
+        loop(0, n_chunks, lambda k: share(k).wait_send())
+        chip_back(False)
+        pass_back(False)
+
+    @pl.when(w == 2)
+    def _():
+        inside(1 - core)
+        loop(0, half, step2)
+        cross(held, None, 0, chip, 0, 2, 0)
+        loop(half, half + 2, step2)
+        shares(0, half)
+        cross(held, None, 0, other, 0, 1, 1)
+        loop(half + 2, half + 4, step2)
+        cross(own_ref, None, 0, other, 0, 1, 2)
+        loop(half + 4, half + 6, step2)
+        cross(own_ref, None, 1, other, 0, 1, 2)
+        loop(half + 6, n_chunks, step2)
+        cross(held, None, 1, chip, 0, 1, 0)
+        loop(n_chunks, n_chunks + 1, step2)
+        cross(held, None, 1, chip, 1, 1, 0)
+        chip_back(True)
+        shares(half, n_chunks)
+        cross(held, None, 0, other, 1, 1, 1)
+        cross(held, None, 1, other, 0, 2, 1)
+        cross(own_ref, None, 0, other, 1, 1, 2)
+        cross(own_ref, None, 1, other, 1, 1, 2)
+        far_back(True)
+        loop(0, n_chunks, lambda k: to_other_partner(k).wait_send())
+        loop(0, n_chunks, lambda k: pass_on(k).wait_send())
+        loop(0, n_chunks, lambda k: share(k).wait_send())
+        chip_back(False)
+        far_back(False)
+
+    @pl.when(w == 3)
+    def _():
+        inside(1 - core)
+        loop(AHEAD, n_chunks, issue)
+        loop(0, n_chunks, lambda k: to_other_partner(k).wait_send())
+        loop(0, n_chunks, lambda k: to_other_left(k).wait_send())
+
+    swap.wait_send()
+    loop(0, 7, lambda i: req_copy(i).wait_send())
+
+    def req_arrived(i):
+        o = (me + 1 + i) % 8
+        remote(req_ref, reqs.at[o], req_send.at[i], req_recv.at[o], grp, o).wait_recv()
+
+    loop(0, 7, req_arrived)
+
+    def best_arrived(i):
+        o = (me + 1 + i) % 8
+        ow = o // 2 + side * (3 - 2 * (o // 2))
+        here = (o == sib) | ((w == 1) & (ow == 0) & (o % 2 == core))
+        here = here | ((w == 2) & (((ow == 1) & (o % 2 == core)) | (ow == 3)))
+
+        @pl.when(jnp.logical_not(here))
+        def _():
+            remote(out_x.at[0, 0], best.at[o], x_send.at[0, 0], best_recv.at[o], grp, o).wait_recv()
+
+    loop(0, 7, best_arrived)
+
+    reqs[me] = req_ref[...]
+    for a in range(2):
+        def one(o, run):
+            mine = req_ref[o]
+            theirs = reqs[o, me]
+            for b in range(2):
+                listed = (mine == b) | (theirs == a)
+                run = jnp.maximum(run, jnp.where(listed, best[o, b * 2 + a], LOW))
+            return run
+        out_ref[a] = lax.fori_loop(0, 8, one, jnp.full((1, BLOCK), LOW, jnp.float32))
+
+
+def pooled(embedding, row_scale, block_rows, requests):
+    blocks_here, width = block_rows.shape[0], embedding.shape[1]
+    rows = blocks_here * BLOCK
+    positions = jnp.arange(BLOCK, dtype=jnp.int32)
+    live = positions[None, :] < block_rows[:, None]
+    decoded = (embedding.astype(jnp.float32) * row_scale[:, None]).astype(jnp.bfloat16)
+    decoded = decoded.reshape(blocks_here, BLOCK, width)
+    decoded = jnp.where(live[:, :, None], decoded, decoded[:, :1, :]).reshape(rows, width)
+    req = jnp.broadcast_to(requests.reshape(8, 1, 1), (8, 1, BLOCK))
+    n = rows // CHUNK
+    dma = pltpu.SemaphoreType.DMA
+    highest = pl.pallas_call(
+        kernel,
+        out_shape=jax.ShapeDtypeStruct((blocks_here, 1, BLOCK), jnp.float32),
+        in_specs=[pl.BlockSpec(memory_space=pltpu.SMEM)] + [pl.BlockSpec(memory_space=pltpu.VMEM)] * 2,
+        out_specs=pl.BlockSpec(memory_space=pltpu.VMEM),
+        scratch_shapes=[
+            pltpu.VMEM((2, rows, width), jnp.bfloat16),
+            pltpu.VMEM((rows, width), jnp.bfloat16),
+            pltpu.VMEM((rows, width), jnp.bfloat16),
+            pltpu.VMEM((2, rows, width), jnp.bfloat16),
+            pltpu.VMEM((8, 4, 1, BLOCK), jnp.float32),
+            pltpu.VMEM((3, 2, 4, 1, BLOCK), jnp.float32),
+            pltpu.VMEM((3, 2, 4, 1, BLOCK), jnp.float32),
+            pltpu.VMEM((8, 8, 1, BLOCK), jnp.int32),
+        ] + [dma((n,))] * 5 + [dma((1,))] + [dma((n,))] * 4 + [
+            dma((2,)), dma((8,)), dma((3, 2)), dma((3, 2)), dma((8,)), dma((8,)),
+        ],
+        compiler_params=pltpu.CompilerParams(
+            collective_id=0, has_side_effects=True, vmem_limit_bytes=40 * 1024 * 1024
+        ),
+    )(block_rows, decoded, req)
+    return jnp.where(live, highest[:, 0, :], jnp.float32(0.0)).reshape(-1)
+
+
 def solution(mesh):
+    small = mesh.shape["grp"] == 4 and mesh.shape["mem"] == 8
     return jax.shard_map(
-        shards,
+        pooled if small else shards,
         mesh=mesh,
         in_specs=(
             P(("grp", "mem"), None),

time: 210 us -> 79.8 us (0.38)
  blocking collectives: 138 us -> 0 us
  Pallas kernels: 0 us -> 75.6 us
  matrix products: 19.3 us -> 0 us
  starting transfers between devices: 14.5 us -> 0 us
  local copies, waits for them, and re-layouts: 13.1 us -> 0.31 us
  other arithmetic: 14.3 us -> 3.61 us
  waiting for transfers between devices: 9.32 us -> 0 us
    unnamed x1 -> x0, blocking collectives: 138 us -> none
    pallas_call x0 -> x1, Pallas kernels: none -> 75.6 us  [pooled(): pl.pallas_call(kernel, out_shape=jax.ShapeDtypeStruct((blocks_here, 1, BL...]
    dot_general x8 -> x0, matrix products: 19.3 us -> none  [visit(): jnp.einsum('arc,sc->ars', decoded, partner, preferred_element_type=jnp.fl...]
    all_to_all x3 -> x0, starting transfers between devices: 14.5 us -> none  [the longest x1 6.33 us: shards(): lax.all_to_all(requests, 'mem', split_axis=1, concat_axis=0, tiled=True)]
    all_to_all x3 -> x0, waiting for transfers between devices: 9.32 us -> none  [the longest x1 5.57 us: shards(): lax.all_to_all(col_best, 'mem', split_axis=0, concat_axis=0, tiled=True)]
    eq x17 -> x0, other arithmetic: 5.25 us -> none  [the longest x8 4.61 us: visit(): diagonal = (local_ids[:, None, None] == own_index) & identity[None, :, :]]
    select_n x4 -> x2, other arithmetic: 6.12 us -> 1.04 us  [the longest x1 0.6 us: pooled(): return jnp.where(live, highest[:, 0, :], jnp.float32(0.0)).reshape(-1)]
    dynamic_slice x16 -> x0, local copies, waits for them, and re-layouts: 4.95 us -> none  [shards(): lax.scan(visit, row_init, (fetched, columns_live, own_block))]
  transfers between devices with their start and end apart: 3 -> 0, of which waited for: 2 -> 0; matrix products, arithmetic and copies ran while one was open for 2% -> 0% of each run, Pallas kernels for 0% -> 0%
where the time goes in v1:
time: 79.8 us; the launch traced here: 79.6 us
  Pallas kernels  75.6 us (95%)
  other arithmetic  3.61 us (5%)
    pallas_call x1, Pallas kernels, pooled(): pl.pallas_call(kernel, out_shape=jax.ShapeDtypeStruct((blocks_here, 1, BL...  75.6 us
    convert_element_type x1, other arithmetic, pooled(): (embedding.astype(jnp.float32) * row_scale[:, None]).astype(jnp.bfloat16)  1.85 us

profile of v1, /device:TPU:0, one launch (start us, length us, event | category | flops | bytes accessed | tf_op | source)
XLA Modules:
  0.0 79.6 jit_solution(5281144412965542277)
XLA Ops:
  0.0 0.7 iota_compare_fusion
  0.7 0.0 copy-start.1
  0.8 0.0 copy-start.2
  0.8 1.8 %multiply_convert_fusion = bf16[1024,768]{1,0:T(8,128)(2,1)S(1)} fusion(bf16[1024,768]{1,0:T(8,128)(2,1)} %param.4, f32[1024]{0:T(1024)} %param.5), kind=kLoop, calls=%fused_computation | loop fusion | flops 2359296 | bytes 3149824 | tf_op jit(solution)/shard_map/convert_element_type | solution.py:379
  2.6 0.0 copy-done.1
  2.7 0.0 copy-done.2
  2.7 0.0 copy-start.3
  2.7 0.0 copy-start
  2.7 0.4 bitcast_select_fusion.own_ref
  3.1 0.2 copy-done.3
  3.3 0.1 broadcast_in_dim.40.req_ref
  3.4 0.0 copy-done
  3.4 75.6 %shard_map.46 = f32[2,1,512]{2,1,0:T(1,128)S(1)} custom-call(s32[2]{0:T(128)S(1)} %copy-done, bf16[1024,768]{1,0:T(8,128)(2,1)S(1)} %bitcast_select_fusion.own_ref, s32[8,1,512]{2,1,0:T(1,128)S(1)} %broadcast_in_dim.40.req_ref), custom_call_target="tpu_custom_call" | custom-call | tf_op jit(solution)/shard_map/pallas_call | solution.py:385
  79.0 0.6 broadcast_select_fusion
  (3 shorter events, 0.0 us)
Async XLA Ops:
  0.7 1.9 %copy-start.1 = (bf16[1024,768]{1,0:T(8,128)(2,1)S(1)}, bf16[1024,768]{1,0:T(8,128)(2,1)}, u32[]{:S(2)}) copy-start(bf16[1024,768]{1,0:T(8,128)(2,1)} %param.4) | copy-start | bytes 4718596
  0.8 1.9 %copy-start.2 = (f32[1024]{0:T(1024)S(1)}, f32[1024]{0:T(1024)}, u32[]{:S(2)}) copy-start(f32[1024]{0:T(1024)} %param.5) | copy-start | bytes 12292
  2.7 0.7 copy-start.3
  2.7 0.7 copy-start

commit v2 on v1

--- a/solution.py
+++ b/solution.py
@@ -6,6 +6,7 @@
 from jax.sharding import PartitionSpec as P
 
 BLOCK = 512
+SUB = 256
 CHUNK = 64
 AHEAD = 4
 LOW = -1e30
@@ -69,7 +70,7 @@
     pgrp = grp + 1 - 2 * side
     sib = me + 1 - 2 * core
     n_chunks = own_ref.shape[0] // CHUNK
-    half = n_chunks // 2
+    per = SUB // CHUNK
 
     def at(group, pos, c):
         s = side if group is grp else 1 - side
@@ -158,28 +159,35 @@
         rows = pl.ds(pl.multiple_of(i * BLOCK, BLOCK), BLOCK)
         return ref[rows, :] if lead is None else ref[lead, rows, :]
 
-    def inside(dev):
-        def one(t):
-            a, b = t % 2, t // 2
-            s = scores_of(block(chip, dev, b), block(chip, core, a))
-            r = lax.broadcasted_iota(jnp.int32, s.shape, 0)
-            c = lax.broadcasted_iota(jnp.int32, s.shape, 1)
-            same = jnp.logical_and(dev == core, a == b).astype(jnp.int32)
-            limit = same * rows_ref[b] + (1 - same) * BLOCK
-            drop = (r >= limit) | ((r - c) * same + (1 - same) == 0)
-            best[dev + me - core, t] = jnp.max(jnp.where(drop, LOW, s), axis=0, keepdims=True)
-        loop(0, 4, one)
-
-    def cross(x, lead, i, ys, j0, n, stage):
-        def one(t):
-            yd, j = t % 2, j0 + t // 2
-            s = scores_of(block(x, lead, i), block(ys, yd, j))
-            out_y[stage, yd, i * 2 + j] = jnp.max(s, axis=0, keepdims=True)
-            m = s[:, :128]
-            for q in range(1, BLOCK // 128):
-                m = jnp.maximum(m, s[:, q * 128:(q + 1) * 128])
-            out_x[stage, yd, j * 2 + i] = jnp.max(m.T, axis=0, keepdims=True)
-        loop(0, 2 * n, one)
+    def inside(dev, t):
+        a, b = t % 2, t // 2
+        s = scores_of(block(chip, dev, b), block(chip, core, a))
+        r = lax.broadcasted_iota(jnp.int32, s.shape, 0)
+        c = lax.broadcasted_iota(jnp.int32, s.shape, 1)
+        same = jnp.logical_and(dev == core, a == b).astype(jnp.int32)
+        limit = same * rows_ref[b] + (1 - same) * BLOCK
+        drop = (r >= limit) | ((r - c) * same + (1 - same) == 0)
+        best[dev + me - core, t] = jnp.max(jnp.where(drop, LOW, s), axis=0, keepdims=True)
+
+    def unit(x, xr, m, ys, yd, yr, n, stage):
+        s = scores_of(x[pl.ds(pl.multiple_of(xr, SUB), m), :], ys[yd, pl.ds(pl.multiple_of(yr, SUB), n), :])
+        i, j = xr // BLOCK, yr // BLOCK
+        xl = pl.ds(pl.multiple_of(xr % BLOCK, SUB), m)
+        yl = pl.ds(pl.multiple_of(yr % BLOCK, SUB), n)
+        col = jnp.max(s, axis=0, keepdims=True)
+        out_y[stage, yd, i * 2 + j, :, yl] = jnp.maximum(out_y[stage, yd, i * 2 + j, :, yl], col)
+        part_max = s[:, :128]
+        for q in range(1, n // 128):
+            part_max = jnp.maximum(part_max, s[:, q * 128:(q + 1) * 128])
+        row = jnp.max(part_max.T, axis=0, keepdims=True)
+        out_x[stage, yd, j * 2 + i, :, xl] = jnp.maximum(out_x[stage, yd, j * 2 + i, :, xl], row)
+
+    def new_rows(x, p, lo, hi):
+        loop(lo, hi, lambda t: unit(x, p * SUB, SUB, chip, t % 2, (t // 2) * BLOCK, BLOCK, 0))
+
+    def new_pairs(x, p):
+        loop(0, 2 * (p + 1), lambda t: unit(x, p * SUB, SUB, other, t % 2, (t // 2) * SUB, SUB, 1))
+        loop(0, 2 * p, lambda t: unit(x, (t // 2) * SUB, SUB, other, t % 2, p * SUB, SUB, 1))
 
     def x_back(stage, group, xid, yid, yd):
         return remote(out_x.at[stage, yd], best.at[yid], x_send.at[stage, yd], best_recv.at[yid], group, xid)
@@ -224,7 +232,7 @@
             to_other_partner(s).wait_recv()
             share(s).start()
 
-        @pl.when(s >= 3)
+        @pl.when((s >= 3) & (s < n_chunks + 3))
         def _():
             pass_on(s - 3).wait_recv()
 
@@ -238,7 +246,7 @@
             to_other_partner(s).wait_recv()
             share(s).start()
 
-        @pl.when(s >= 2)
+        @pl.when((s >= 2) & (s < n_chunks + 2))
         def _():
             pass_on(s - 2).wait_recv()
             pass_on(s - 2).start()
@@ -246,7 +254,7 @@
     def step2(s):
         issue(s + AHEAD)
 
-        @pl.when(s >= 1)
+        @pl.when((s >= 1) & (s < n_chunks + 1))
         def _():
             pass_held(s - 1).wait_recv()
             pass_on(s - 1).start()
@@ -257,21 +265,51 @@
             share(s).start()
             to_held(s).wait_recv()
 
+    def work0(t, p):
+        if t == 3:
+            shares(p * per, (p + 1) * per)
+            new_pairs(passing, p)
+
+    def work1(t, p):
+        if t < 2:
+            new_rows(held, p, 2 * t, 2 * t + 2)
+        elif t == 3:
+            shares(p * per, (p + 1) * per)
+            new_pairs(passing, p)
+
+    def work2(t, p):
+        if t == 0:
+            new_rows(held, p, 0, 4)
+        elif t < 3:
+            if t == 1:
+                shares(p * per, (p + 1) * per)
+            loop(0, 2, lambda y: unit(own_ref, (t - 1) * BLOCK, BLOCK, other, y, p * SUB, SUB, 2))
+        else:
+            new_pairs(held, p)
+
+    def phases(step, work):
+        def phase(p):
+            for t in range(per):
+                step(p * per + t)
+
+                @pl.when(p == 0)
+                def _():
+                    inside(core, t)
+                    inside(1 - core, t)
+
+                @pl.when(p > 0)
+                def _():
+                    work(t, p - 1)
+        loop(0, n_chunks // per + 1, phase)
+
+    out_x[...] = jnp.full(out_x.shape, LOW, out_x.dtype)
+    out_y[...] = jnp.full(out_y.shape, LOW, out_y.dtype)
     local.wait()
-    inside(core)
     swapped.wait_recv()
 
     @pl.when(w == 0)
     def _():
-        inside(1 - core)
-        loop(0, half + 4, step0)
-        shares(0, half)
-        cross(passing, None, 0, other, 0, 1, 1)
-        loop(half + 4, n_chunks + 1, step0)
-        shares(half, n_chunks)
-        cross(passing, None, 0, other, 1, 1, 1)
-        loop(n_chunks + 1, n_chunks + 3, step0)
-        cross(passing, None, 1, other, 0, 2, 1)
+        phases(step0, work0)
         pass_back(True)
         loop(0, n_chunks, lambda k: to_held(k).wait_send())
         loop(0, n_chunks, lambda k: share(k).wait_send())
@@ -279,21 +317,8 @@
 
     @pl.when(w == 1)
     def _():
-        inside(1 - core)
-        loop(0, half, step1)
-        cross(held, None, 0, chip, 0, 2, 0)
-        loop(half, half + 4, step1)
-        shares(0, half)
-        cross(passing, None, 0, other, 0, 1, 1)
-        loop(half + 4, n_chunks, step1)
-        cross(held, None, 1, chip, 0, 1, 0)
-        loop(n_chunks, n_chunks + 1, step1)
-        cross(held, None, 1, chip, 1, 1, 0)
+        phases(step1, work1)
         chip_back(True)
-        loop(n_chunks + 1, n_chunks + 2, step1)
-        shares(half, n_chunks)
-        cross(passing, None, 0, other, 1, 1, 1)
-        cross(passing, None, 1, other, 0, 2, 1)
         pass_back(True)
         loop(0, n_chunks, lambda k: to_held(k).wait_send())
         loop(0, n_chunks, lambda k: pass_held(k).wait_send())
@@ -304,26 +329,8 @@
 
     @pl.when(w == 2)
     def _():
-        inside(1 - core)
-        loop(0, half, step2)
-        cross(held, None, 0, chip, 0, 2, 0)
-        loop(half, half + 2, step2)
-        shares(0, half)
-        cross(held, None, 0, other, 0, 1, 1)
-        loop(half + 2, half + 4, step2)
-        cross(own_ref, None, 0, other, 0, 1, 2)
-        loop(half + 4, half + 6, step2)
-        cross(own_ref, None, 1, other, 0, 1, 2)
-        loop(half + 6, n_chunks, step2)
-        cross(held, None, 1, chip, 0, 1, 0)
-        loop(n_chunks, n_chunks + 1, step2)
-        cross(held, None, 1, chip, 1, 1, 0)
+        phases(step2, work2)
         chip_back(True)
-        shares(half, n_chunks)
-        cross(held, None, 0, other, 1, 1, 1)
-        cross(held, None, 1, other, 0, 2, 1)
-        cross(own_ref, None, 0, other, 1, 1, 2)
-        cross(own_ref, None, 1, other, 1, 1, 2)
         far_back(True)
         loop(0, n_chunks, lambda k: to_other_partner(k).wait_send())
         loop(0, n_chunks, lambda k: pass_on(k).wait_send())
@@ -333,8 +340,9 @@
 
     @pl.when(w == 3)
     def _():
-        inside(1 - core)
         loop(AHEAD, n_chunks, issue)
+        loop(0, 4, lambda t: inside(core, t))
+        loop(0, 4, lambda t: inside(1 - core, t))
         loop(0, n_chunks, lambda k: to_other_partner(k).wait_send())
         loop(0, n_chunks, lambda k: to_other_left(k).wait_send())
 

time: 79.8 us -> 85.5 us (1.071)
  Pallas kernels: 75.6 us -> 81.4 us
    pallas_call x1, Pallas kernels: 75.6 us -> 81.4 us  [pooled(): pl.pallas_call(kernel, out_shape=jax.ShapeDtypeStruct((blocks_here, 1, BL...]
where the time goes in v2:
time: 85.5 us; the launch traced here: 85.4 us
  Pallas kernels  81.4 us (95%)
  other arithmetic  3.61 us (4%)
    pallas_call x1, Pallas kernels, pooled(): pl.pallas_call(kernel, out_shape=jax.ShapeDtypeStruct((blocks_here, 1, BL...  81.4 us
    convert_element_type x1, other arithmetic, pooled(): (embedding.astype(jnp.float32) * row_scale[:, None]).astype(jnp.bfloat16)  1.85 us

profile of v2, /device:TPU:0, one launch (start us, length us, event | category | flops | bytes accessed | tf_op | source)
XLA Modules:
  0.0 85.4 jit_solution(11685202966363454697)
XLA Ops:
  0.0 0.7 iota_compare_fusion
  0.7 0.0 copy-start.1
  0.8 0.0 copy-start.2
  0.8 1.8 %multiply_convert_fusion = bf16[1024,768]{1,0:T(8,128)(2,1)S(1)} fusion(bf16[1024,768]{1,0:T(8,128)(2,1)} %param.4, f32[1024]{0:T(1024)} %param.5), kind=kLoop, calls=%fused_computation | loop fusion | flops 2359296 | bytes 3149824 | tf_op jit(solution)/shard_map/convert_element_type | solution.py:387
  2.6 0.0 copy-done.1
  2.7 0.0 copy-done.2
  2.7 0.0 copy-start.3
  2.7 0.0 copy-start
  2.7 0.4 bitcast_select_fusion.own_ref
  3.1 0.2 copy-done.3
  3.3 0.1 broadcast_in_dim.40.req_ref
  3.4 0.0 copy-done
  3.4 81.4 %shard_map.46 = f32[2,1,512]{2,1,0:T(1,128)S(1)} custom-call(s32[2]{0:T(128)S(1)} %copy-done, bf16[1024,768]{1,0:T(8,128)(2,1)S(1)} %bitcast_select_fusion.own_ref, s32[8,1,512]{2,1,0:T(1,128)S(1)} %broadcast_in_dim.40.req_ref), custom_call_target="tpu_custom_call" | custom-call | tf_op jit(solution)/shard_map/pallas_call | solution.py:393
  84.8 0.6 broadcast_select_fusion
  (3 shorter events, 0.0 us)
Async XLA Ops:
  0.7 1.9 %copy-start.1 = (bf16[1024,768]{1,0:T(8,128)(2,1)S(1)}, bf16[1024,768]{1,0:T(8,128)(2,1)}, u32[]{:S(2)}) copy-start(bf16[1024,768]{1,0:T(8,128)(2,1)} %param.4) | copy-start | bytes 4718596
  0.8 1.9 %copy-start.2 = (f32[1024]{0:T(1024)S(1)}, f32[1024]{0:T(1024)}, u32[]{:S(2)}) copy-start(f32[1024]{0:T(1024)} %param.5) | copy-start | bytes 12292
  2.7 0.7 copy-start.3
  2.7 0.7 copy-start

commit v3 on v1

--- a/solution.py
+++ b/solution.py
@@ -113,6 +113,9 @@
     def pass_held(k):
         return remote(held.at[part(k)], passing.at[part(k)], held_send.at[k], passing_recv.at[k], pgrp, me)
 
+    def hop(k):
+        return remote(held.at[part(k)], held.at[part(k)], held_send.at[k], held_recv.at[k], grp, at(grp, 3, core))
+
     def pass_on(k):
         return remote(passing.at[part(k)], passing.at[part(k)], passing_send.at[k], passing_recv.at[k], grp, at(grp, w - 1, core))
 
@@ -187,8 +190,8 @@
     def y_back(stage, group, xid, yid, yd):
         return remote(out_y.at[stage, yd], best.at[xid], y_send.at[stage, yd], best_recv.at[xid], group, yid)
 
-    def chip_back(start):
-        xid = at(grp, w - 1, core)
+    def chip_back(start, pos):
+        xid = at(grp, pos, core)
         ops = [x_back(0, grp, xid, at(grp, w, yd), yd) for yd in range(2)]
         ops.append(y_back(0, grp, xid, sib, 1 - core))
         for op in ops:
@@ -204,12 +207,10 @@
                 op.start() if start else op.wait_send()
 
     def far_back(start):
-        xid = at(grp, 1, core)
         for yd in range(2):
             yid = at(grp, 3, yd)
-            ops = (x_back(1, grp, xid, yid, yd), y_back(1, grp, xid, yid, yd), y_back(2, grp, me, yid, yd))
-            for op in ops:
-                op.start() if start else op.wait_send()
+            op = y_back(2, grp, me, yid, yd)
+            op.start() if start else op.wait_send()
             if start:
                 best[yid] = out_x[2, yd]
 
@@ -256,6 +257,11 @@
             to_other_left(s).wait_recv()
             share(s).start()
             to_held(s).wait_recv()
+            hop(s).start()
+
+    def step3(s):
+        issue(s + AHEAD)
+        hop(s).wait_recv()
 
     local.wait()
     inside(core)
@@ -263,8 +269,9 @@
 
     @pl.when(w == 0)
     def _():
+        loop(0, half, step0)
         inside(1 - core)
-        loop(0, half + 4, step0)
+        loop(half, half + 4, step0)
         shares(0, half)
         cross(passing, None, 0, other, 0, 1, 1)
         loop(half + 4, n_chunks + 1, step0)
@@ -279,64 +286,60 @@
 
     @pl.when(w == 1)
     def _():
-        inside(1 - core)
         loop(0, half, step1)
         cross(held, None, 0, chip, 0, 2, 0)
         loop(half, half + 4, step1)
         shares(0, half)
         cross(passing, None, 0, other, 0, 1, 1)
-        loop(half + 4, n_chunks, step1)
-        cross(held, None, 1, chip, 0, 1, 0)
-        loop(n_chunks, n_chunks + 1, step1)
-        cross(held, None, 1, chip, 1, 1, 0)
-        chip_back(True)
-        loop(n_chunks + 1, n_chunks + 2, step1)
+        loop(half + 4, n_chunks + 2, step1)
         shares(half, n_chunks)
         cross(passing, None, 0, other, 1, 1, 1)
         cross(passing, None, 1, other, 0, 2, 1)
         pass_back(True)
+        cross(held, None, 1, chip, 0, 2, 0)
+        chip_back(True, 0)
+        inside(1 - core)
         loop(0, n_chunks, lambda k: to_held(k).wait_send())
         loop(0, n_chunks, lambda k: pass_held(k).wait_send())
         loop(0, n_chunks, lambda k: pass_on(k).wait_send())
         loop(0, n_chunks, lambda k: share(k).wait_send())
-        chip_back(False)
+        chip_back(False, 0)
         pass_back(False)
 
     @pl.when(w == 2)
     def _():
-        inside(1 - core)
         loop(0, half, step2)
         cross(held, None, 0, chip, 0, 2, 0)
-        loop(half, half + 2, step2)
+        loop(half, half + 4, step2)
         shares(0, half)
-        cross(held, None, 0, other, 0, 1, 1)
-        loop(half + 2, half + 4, step2)
         cross(own_ref, None, 0, other, 0, 1, 2)
-        loop(half + 4, half + 6, step2)
+        loop(half + 4, n_chunks + 1, step2)
+        cross(held, None, 1, chip, 0, 2, 0)
+        chip_back(True, 1)
         cross(own_ref, None, 1, other, 0, 1, 2)
-        loop(half + 6, n_chunks, step2)
-        cross(held, None, 1, chip, 0, 1, 0)
-        loop(n_chunks, n_chunks + 1, step2)
-        cross(held, None, 1, chip, 1, 1, 0)
-        chip_back(True)
         shares(half, n_chunks)
-        cross(held, None, 0, other, 1, 1, 1)
-        cross(held, None, 1, other, 0, 2, 1)
         cross(own_ref, None, 0, other, 1, 1, 2)
         cross(own_ref, None, 1, other, 1, 1, 2)
         far_back(True)
+        inside(1 - core)
         loop(0, n_chunks, lambda k: to_other_partner(k).wait_send())
+        loop(0, n_chunks, lambda k: hop(k).wait_send())
         loop(0, n_chunks, lambda k: pass_on(k).wait_send())
         loop(0, n_chunks, lambda k: share(k).wait_send())
-        chip_back(False)
+        chip_back(False, 1)
         far_back(False)
 
     @pl.when(w == 3)
     def _():
+        loop(0, half, step3)
         inside(1 - core)
-        loop(AHEAD, n_chunks, issue)
+        cross(held, None, 0, chip, 0, 2, 0)
+        loop(half, n_chunks, step3)
+        cross(held, None, 1, chip, 0, 2, 0)
+        chip_back(True, 1)
         loop(0, n_chunks, lambda k: to_other_partner(k).wait_send())
         loop(0, n_chunks, lambda k: to_other_left(k).wait_send())
+        chip_back(False, 1)
 
     swap.wait_send()
     loop(0, 7, lambda i: req_copy(i).wait_send())
@@ -351,6 +354,7 @@
         o = (me + 1 + i) % 8
         ow = o // 2 + side * (3 - 2 * (o // 2))
         here = (o == sib) | ((w == 1) & (ow == 0) & (o % 2 == core))
+        here = here | ((w == 3) & (ow == 1) & (o % 2 == core))
         here = here | ((w == 2) & (((ow == 1) & (o % 2 == core)) | (ow == 3)))
 
         @pl.when(jnp.logical_not(here))

time: 79.8 us -> 77 us (0.965)
  Pallas kernels: 75.6 us -> 72.8 us
    pallas_call x1, Pallas kernels: 75.6 us -> 72.8 us  [pooled(): pl.pallas_call(kernel, out_shape=jax.ShapeDtypeStruct((blocks_here, 1, BL...]
where the time goes in v3:
time: 77 us; the launch traced here: 76.8 us
  Pallas kernels  72.8 us (95%)
  other arithmetic  3.61 us (5%)
    pallas_call x1, Pallas kernels, pooled(): pl.pallas_call(kernel, out_shape=jax.ShapeDtypeStruct((blocks_here, 1, BL...  72.8 us
    convert_element_type x1, other arithmetic, pooled(): (embedding.astype(jnp.float32) * row_scale[:, None]).astype(jnp.bfloat16)  1.85 us

profile of v3, /device:TPU:0, one launch (start us, length us, event | category | flops | bytes accessed | tf_op | source)
XLA Modules:
  0.0 76.8 jit_solution(7734367734772055233)
XLA Ops:
  0.0 0.7 iota_compare_fusion
  0.7 0.0 copy-start.1
  0.8 0.0 copy-start.2
  0.8 1.8 %multiply_convert_fusion = bf16[1024,768]{1,0:T(8,128)(2,1)S(1)} fusion(bf16[1024,768]{1,0:T(8,128)(2,1)} %param.4, f32[1024]{0:T(1024)} %param.5), kind=kLoop, calls=%fused_computation | loop fusion | flops 2359296 | bytes 3149824 | tf_op jit(solution)/shard_map/convert_element_type | solution.py:383
  2.6 0.0 copy-done.1
  2.7 0.0 copy-done.2
  2.7 0.0 copy-start.3
  2.7 0.0 copy-start
  2.7 0.4 bitcast_select_fusion.own_ref
  3.1 0.2 copy-done.3
  3.3 0.1 broadcast_in_dim.40.req_ref
  3.4 0.0 copy-done
  3.4 72.8 %shard_map.46 = f32[2,1,512]{2,1,0:T(1,128)S(1)} custom-call(s32[2]{0:T(128)S(1)} %copy-done, bf16[1024,768]{1,0:T(8,128)(2,1)S(1)} %bitcast_select_fusion.own_ref, s32[8,1,512]{2,1,0:T(1,128)S(1)} %broadcast_in_dim.40.req_ref), custom_call_target="tpu_custom_call" | custom-call | tf_op jit(solution)/shard_map/pallas_call | solution.py:389
  76.3 0.6 broadcast_select_fusion
  (3 shorter events, 0.0 us)
Async XLA Ops:
  0.7 1.9 %copy-start.1 = (bf16[1024,768]{1,0:T(8,128)(2,1)S(1)}, bf16[1024,768]{1,0:T(8,128)(2,1)}, u32[]{:S(2)}) copy-start(bf16[1024,768]{1,0:T(8,128)(2,1)} %param.4) | copy-start | bytes 4718596
  0.8 1.9 %copy-start.2 = (f32[1024]{0:T(1024)S(1)}, f32[1024]{0:T(1024)}, u32[]{:S(2)}) copy-start(f32[1024]{0:T(1024)} %param.5) | copy-start | bytes 12292
  2.7 0.7 copy-start.3
  2.7 0.7 copy-start
